TPU v7x, 32 devices: a whole 2x2x4 slice. The times are simulated.
32 devices in a mesh: stn: 16 (over z, y, x), chan: 2 (over core).
Axes of the slice: x: 2, y: 2, z: 4, core: 2. Of those that a mesh axis runs over, the one named last changes fastest.
Arguments:
- voltages: bfloat16 [128, 4, 64, 128], P('stn', 'chan'), may hold values from -12 to 12
- response: bfloat16 [128, 4, 64, 128], P('stn', 'chan'), may hold values from -48 to 48
- start_gains: float32 [128, 128], replicated, may hold values from 0.5 to 1.5
- step_sizes: float32 [64], replicated, may hold values from 0.2 to 0.8
- station_ids: int32 [128], P('stn'), may hold values from 0 to 127, each once
- baseline_flags: int32 [128, 128], replicated, may hold values 0 or 1
Outputs:
- calibrated: float32 [128, 128], P('stn')
- descent: float32 [128, 128], P('stn')
Inputs may be any that keep to these rules, and one draw needn't show every extreme that they name: `station_ids`: each station number appears once. `baseline_flags`: 1 keeps a baseline, 0 flags it.
All inputs are finite; a program needn't handle non-finite values.
Results may differ from a plain program's by a relative error of at most 0.0003.
Values may be sent and summed in bfloat16 or wider, within the bound.
A program may use at most 64 MiB of HBM per device.

v0:
```python
import functools

import jax
import jax.numpy as jnp
from jax import lax
from jax.experimental import pallas as pl
from jax.experimental.pallas import tpu as pltpu
from jax.sharding import PartitionSpec as P

ITERS = 2
MESH = pl.DeviceIdType.MESH
IDS, RESP, VOLT, SUMS, GATHER = 0, 1, 2, 4, 4 + ITERS
NORM = GATHER + ITERS
GROUPS = NORM + 1


def dot_last(left, right):
    return lax.dot_general(left, right, (((1,), (1,)), ((), ())), preferred_element_type=jnp.float32)


def dot(left, right):
    return lax.dot_general(left, right, (((1,), (0,)), ((), ())), preferred_element_type=jnp.float32)


def kernel(
    n, nchan, stations, samples,
    volt_any, resp_any, gains_any, steps_any, ids_any, flags_any,
    calibrated_ref, descent_ref,
    volt_in, resp_in, gains, flags, wide_volt, wide_resp,
    volt_send, resp_send, volt_recv, resp_recv, id_rows,
    weight, a_float, a_swap, applied, observed, diff,
    energy_out, sums, gathered, norms, current, steps_ref, ids_ref,
    in_sem, send_sem, recv_sem,
):
    everyone = n * stations
    devices = n * nchan
    spd = samples // n
    rows = stations // nchan
    width = volt_in.shape[2]
    half = width // 2
    stn = lax.axis_index("stn")
    chan = lax.axis_index("chan")
    me = stn * nchan + chan

    def each(first, stop, body):
        if stop - first <= 16:
            for k in range(first, stop):
                body(k)
        else:
            lax.fori_loop(first, stop, lambda k, carry: (body(k), carry)[1], 0)

    def other_stations(body):
        each(1, n, lambda k: body(lax.rem(stn + k, n)))

    def other_devices(body):
        each(1, n, lambda k: [body(lax.rem(stn + k, n), lax.rem(chan + c, nchan)) for c in range(nchan)])
        for c in range(1, nchan):
            body(stn, lax.rem(chan + c, nchan))

    loads = [
        pltpu.make_async_copy(src, dst, in_sem.at[i])
        for i, (src, dst) in enumerate(
            (
                (ids_any, ids_ref), (resp_any, resp_in), (volt_any, volt_in),
                (flags_any, flags), (gains_any, gains), (steps_any, steps_ref),
            )
        )
    ]
    for load in loads:
        load.start()

    barrier = pltpu.get_barrier_semaphore()

    def greet(s, c):
        pl.semaphore_signal(barrier, inc=1, device_id={"stn": s, "chan": c}, device_id_type=MESH)

    other_devices(greet)

    def wait_all(buffer, count, sem):
        part = buffer.at[pl.ds(0, count)]
        pltpu.make_async_copy(part, part, sem).wait()

    loads[0].wait()
    lane = lax.broadcasted_iota(jnp.int32, (1, everyone), 1)
    own_row = jnp.zeros((1, everyone), jnp.int32)
    for j in range(stations):
        own_row = jnp.where(lane == stn * stations + j, ids_ref[j], own_row)
    id_rows[stn] = own_row

    loads[1].wait()
    wide_resp[...] = resp_in[...].astype(jnp.float32).reshape(stations * samples, width)

    def pack(wide, send, dst, pairs):
        for pair in pairs:
            first = dst * spd + 2 * pair
            both = jnp.concatenate(
                [wide[pl.ds(first + j, stations, stride=samples), :] for j in range(2)], axis=0
            )
            send[dst, pl.ds(2 * pair * stations, 2 * stations), :] = both.astype(jnp.bfloat16)

    def remote(src, dst_ref, group, device):
        pltpu.make_async_remote_copy(
            src_ref=src, dst_ref=dst_ref, send_sem=send_sem.at[group],
            recv_sem=recv_sem.at[group], device_id=device, device_id_type=MESH,
        ).start()

    pairs = spd // 2
    chunks = 2 if pairs % 2 == 0 else 1
    chunk_pairs = [range(c * pairs // chunks, (c + 1) * pairs // chunks) for c in range(chunks)]
    chunk_rows = [
        pl.ds(2 * part.start * stations, 2 * len(part) * stations) for part in chunk_pairs
    ]

    pl.semaphore_wait(barrier, devices - 1)

    def send_resp(dst):
        remote(id_rows.at[stn], id_rows.at[stn], IDS, {"stn": dst})
        pack(wide_resp, resp_send, dst, range(pairs))
        remote(resp_send.at[dst], resp_recv.at[stn], RESP, {"stn": dst})

    other_stations(send_resp)
    loads[2].wait()
    wide_volt[...] = volt_in[...].astype(jnp.float32).reshape(stations * samples, width)
    for chunk in range(chunks):

        def send_volt(dst, chunk=chunk):
            pack(wide_volt, volt_send, dst, chunk_pairs[chunk])
            part = chunk_rows[chunk]
            remote(volt_send.at[dst, part], volt_recv.at[stn, part], VOLT + chunk, {"stn": dst})

        other_stations(send_volt)
    pack(wide_resp, resp_send, stn, range(pairs))
    resp_recv[stn] = resp_send[stn]
    pack(wide_volt, volt_send, stn, range(pairs))
    volt_recv[stn] = volt_send[stn]

    loads[3].wait()
    flag = flags[...].astype(jnp.float32)
    mutual = (flag * flag.T).astype(jnp.bfloat16)
    wait_all(id_rows, n - 1, recv_sem.at[IDS])
    all_ids = jnp.sum(id_rows[...], axis=0)
    row = lax.broadcasted_iota(jnp.int32, (everyone, everyone), 0)
    column = lax.broadcasted_iota(jnp.int32, (everyone, everyone), 1)
    one_hot = (row == all_ids).astype(jnp.float32).astype(jnp.bfloat16)
    picked = dot(mutual, one_hot).T.astype(jnp.bfloat16)
    weight[...] = jnp.where(row == column, 0.0, dot(picked, one_hot))

    def unpack(recv, pair):
        block = recv[:, pl.ds(2 * pair * stations, 2 * stations), :].astype(jnp.float32)
        block = block.reshape(n, 2, stations, width)
        return [block[:, j].reshape(everyone, width) for j in range(2)]

    sign = jnp.where(lax.broadcasted_iota(jnp.int32, (1, width), 1) < half, -1.0, 1.0)
    loads[4].wait()
    loads[5].wait()
    steps = steps_ref[...].reshape(1, half)
    steps = jnp.concatenate([steps, steps], axis=1)

    def predict(t, gain_both, gain_turn):
        a = a_float[t]
        turned = gain_both * a + gain_turn * a_swap[t]
        applied[t, pl.ds(0, everyone), :] = turned.astype(jnp.bfloat16)
        applied[t, pl.ds(everyone, everyone), :] = (sign * pltpu.roll(turned, half, 1)).astype(jnp.bfloat16)
        return dot_last(applied[t, pl.ds(0, everyone), :], applied[t])

    def gain_parts(gain):
        swapped = pltpu.roll(gain, half, 1)
        left = sign < 0.0
        return jnp.where(left, gain, swapped), jnp.where(left, -swapped, gain)

    wait_all(resp_recv, n - 1, recv_sem.at[RESP])
    gain_both, gain_turn = gain_parts(gains[...])
    for pair in range(spd // 2):
        for j, a in enumerate(unpack(resp_recv, pair)):
            t = 2 * pair + j
            a_float[t] = a
            a_swap[t] = pltpu.roll(a, half, 1)
            diff[t] = predict(t, gain_both, gain_turn)

    def accumulate(t, totals):
        residual = jnp.concatenate(
            [
                (weight[...] * diff[t, :, pl.ds(0, everyone)]).astype(jnp.bfloat16),
                (weight[...] * diff[t, :, pl.ds(everyone, everyone)]).astype(jnp.bfloat16),
            ],
            axis=1,
        )
        hidden = dot(residual, applied[t])
        return totals[0] + a_float[t] * hidden, totals[1] + a_swap[t] * hidden

    def volt_chunk(chunk):
        part = volt_recv.at[pl.ds(0, n - 1), chunk_rows[chunk]]
        return pltpu.make_async_copy(part, part, recv_sem.at[VOLT + chunk])

    for iteration in range(ITERS):
        totals = (jnp.zeros((everyone, width), jnp.float32), jnp.zeros((everyone, width), jnp.float32))
        if iteration == 0:
            for chunk in range(chunks):
                volt_chunk(chunk).wait()
                for pair in chunk_pairs[chunk]:
                    for j, x in enumerate(unpack(volt_recv, pair)):
                        t = 2 * pair + j
                        mine = x.astype(jnp.bfloat16)
                        turned = (sign * pltpu.roll(x, half, 1)).astype(jnp.bfloat16)
                        seen = dot_last(mine, jnp.concatenate([mine, turned], axis=0))
                        observed[t] = seen
                        diff[t] = seen - diff[t]
                        totals = accumulate(t, totals)
        else:
            gain_both, gain_turn = gain_parts(current[...])
            for t in range(spd):
                diff[t] = observed[t] - predict(t, gain_both, gain_turn)
                totals = accumulate(t, totals)
        direct, crossed = totals
        energy = jnp.where(
            sign < 0.0,
            direct + pltpu.roll(direct, half, 1),
            crossed - pltpu.roll(crossed, half, 1),
        )
        energy_out[iteration] = energy.reshape(devices, rows, width)

        def send_sum(s, c):
            remote(
                energy_out.at[iteration, s * nchan + c], sums.at[iteration, me],
                SUMS + iteration, {"stn": s, "chan": c},
            )

        other_devices(send_sum)
        sums[iteration, me] = energy_out[iteration, me]
        wait_all(sums.at[iteration], devices - 1, recv_sem.at[SUMS + iteration])
        scale = -(2.0 / half) / half
        block = scale * jnp.sum(sums[iteration], axis=0)
        gathered[iteration, me] = block
        if iteration < ITERS - 1:

            def send_block(s, c):
                mine = gathered.at[iteration, me]
                remote(mine, mine, GATHER + iteration, {"stn": s, "chan": c})

            other_devices(send_block)
            wait_all(gathered.at[iteration], devices - 1, recv_sem.at[GATHER + iteration])
            gradient = gathered[iteration].reshape(everyone, width)
            spread = jnp.sqrt(jnp.sum(gradient * gradient, keepdims=True) / (everyone * half) + 1e-06)
            held = gains if iteration == 0 else current
            current[...] = held[...] - steps * (gradient / spread)
        else:
            norms[me] = jnp.sum(block * block, axis=0, keepdims=True)

            def send_norm(s, c):
                remote(norms.at[me], norms.at[me], NORM, {"stn": s, "chan": c})

            for c in range(1, nchan):
                mine = gathered.at[iteration, me]
                remote(mine, mine, GATHER + iteration, {"chan": lax.rem(chan + c, nchan)})
            other_devices(send_norm)
            wait_all(gathered.at[iteration], nchan - 1, recv_sem.at[GATHER + iteration])
            gradient = gathered[iteration, pl.ds(stn * nchan, nchan)].reshape(stations, width)
            own = current[pl.ds(pl.multiple_of(stn * stations, stations), stations), :]
            wait_all(norms, devices - 1, recv_sem.at[NORM])
            total = jnp.sum(jnp.sum(norms[...], axis=0), keepdims=True)
            spread = jnp.sqrt(total / (everyone * half) + 1e-06)
            descent = gradient / spread
            calibrated_ref[...] = own - steps * descent
            descent_ref[...] = descent

    wait_all(id_rows, n - 1, send_sem.at[IDS])
    wait_all(resp_send, n - 1, send_sem.at[RESP])
    for chunk in range(chunks):
        part = volt_send.at[pl.ds(0, n - 1), chunk_rows[chunk]]
        pltpu.make_async_copy(part, part, send_sem.at[VOLT + chunk]).wait()
    for iteration in range(ITERS):
        wait_all(sums.at[iteration], devices - 1, send_sem.at[SUMS + iteration])
        count = devices - 1 if iteration < ITERS - 1 else nchan - 1
        wait_all(gathered.at[iteration], count, send_sem.at[GATHER + iteration])
    wait_all(norms, devices - 1, send_sem.at[NORM])


def shards(n, nchan, voltages, response, start_gains, step_sizes, station_ids, baseline_flags):
    stations, width = voltages.shape[0], voltages.shape[3]
    samples = voltages.shape[1] * voltages.shape[2]
    everyone = stations * n
    devices = n * nchan
    spd = samples // n
    half = width // 2
    rows = stations // nchan
    f32, bf16 = jnp.float32, jnp.bfloat16
    hbm = pl.BlockSpec(memory_space=pltpu.HBM)
    vmem = pl.BlockSpec(memory_space=pltpu.VMEM)
    block = (n, spd * stations, width)
    scratch = [
        ((stations, samples, width), bf16),
        ((stations, samples, width), bf16),
        ((everyone, width), f32),
        ((everyone, everyone), jnp.int32),
        ((stations * samples, width), f32),
        ((stations * samples, width), f32),
        (block, bf16),
        (block, bf16),
        (block, bf16),
        (block, bf16),
        ((n, 1, everyone), jnp.int32),
        ((everyone, everyone), f32),
        ((spd, everyone, width), f32),
        ((spd, everyone, width), f32),
        ((spd, 2 * everyone, width), bf16),
        ((spd, everyone, 2 * everyone), f32),
        ((spd, everyone, 2 * everyone), f32),
        ((ITERS, devices, rows, width), f32),
        ((ITERS, devices, rows, width), f32),
        ((ITERS, devices, rows, width), f32),
        ((devices, 1, width), f32),
        ((everyone, width), f32),
        ((half,), f32),
    ]
    return pl.pallas_call(
        functools.partial(kernel, n, nchan, stations, samples),
        out_shape=[jax.ShapeDtypeStruct((stations, width), f32)] * 2,
        in_specs=[hbm] * 6,
        out_specs=[vmem, vmem],
        scratch_shapes=[pltpu.VMEM(shape, dtype) for shape, dtype in scratch]
        + [pltpu.SMEM((stations,), jnp.int32), pltpu.SemaphoreType.DMA((6,)), pltpu.SemaphoreType.DMA((GROUPS,)), pltpu.SemaphoreType.DMA((GROUPS,))],
        compiler_params=pltpu.CompilerParams(
            collective_id=0, has_side_effects=True, vmem_limit_bytes=48 * 1024 * 1024
        ),
    )(
        voltages.reshape(stations, samples, width),
        response.reshape(stations, samples, width),
        start_gains, step_sizes, station_ids, baseline_flags,
    )


def solution(mesh):
    placed = (P("stn", "chan", None, None), P("stn", "chan", None, None), P(), P(), P("stn"), P())
    return jax.shard_map(
        functools.partial(shards, mesh.shape["stn"], mesh.shape["chan"]),
        mesh=mesh,
        in_specs=placed,
        out_specs=(P("stn", None), P("stn", None)),
        check_vma=False,
    )
```

profile of v0, /device:TPU:0, one launch (start us, length us, event | category | flops | bytes accessed | tf_op | source)
XLA Modules:
  0.0 46.2 jit_solution(12469070294717892424)
XLA Ops:
  0.6 0.0 copy-start.4
  0.6 0.0 copy-start.5
  0.7 0.6 %copy-done.4 = f32[64]{0:T(128)S(1)} copy-done((f32[64]{0:T(128)S(1)}, f32[64]{0:T(128)}, u32[]{:S(2)}) %copy-start.4) | copy-done | bytes 280
  1.3 0.0 copy-done.5
  1.3 0.0 copy-start
  1.3 0.9 %copy-done = bf16[8,2,64,128]{3,2,1,0:T(8,128)(2,1)S(1)} copy-done((bf16[8,2,64,128]{3,2,1,0:T(8,128)(2,1)S(1)}, bf16[8,2,64,128]{3,2,1,0:T(8,128)(2,1)}, u32[]{:S(2)}) %copy-start) | copy-done | bytes 262168
  2.3 0.0 copy-start.1
  2.3 0.9 %copy-done.1 = bf16[8,2,64,128]{3,2,1,0:T(8,128)(2,1)S(1)} copy-done((bf16[8,2,64,128]{3,2,1,0:T(8,128)(2,1)S(1)}, bf16[8,2,64,128]{3,2,1,0:T(8,128)(2,1)}, u32[]{:S(2)}) %copy-start.1) | copy-done | bytes 262168
  3.2 0.0 copy-start.2
  3.2 0.8 %copy-done.2 = f32[128,128]{1,0:T(8,128)S(1)} copy-done((f32[128,128]{1,0:T(8,128)S(1)}, f32[128,128]{1,0:T(8,128)}, u32[]{:S(2)}) %copy-start.2) | copy-done | bytes 65560
  4.0 0.0 copy-start.3
  4.0 0.8 %copy-done.3 = s32[128,128]{1,0:T(8,128)S(1)} copy-done((s32[128,128]{1,0:T(8,128)S(1)}, s32[128,128]{1,0:T(8,128)}, u32[]{:S(2)}) %copy-start.3) | copy-done | bytes 65560
  4.9 40.1 %shard_map.77 = (f32[8,128]{1,0:T(8,128)S(1)}, f32[8,128]{1,0:T(8,128)S(1)}) custom-call(bf16[8,128,128]{2,1,0:T(8,128)(2,1)S(1)} %bitcast.2, bf16[8,128,128]{2,1,0:T(8,128)(2,1)S(1)} %bitcast.3, f32[128,128]{1,0:T(8,128)S(1)} %copy-done.2, f32[64]{0:T(128)S(1)} %copy-done.4, s32[8]{0:T(128)S(1)} %copy-done.5, s32[128,128]{1,0:T(8,128)S(1)} %copy-done.3), custom_call_target="tpu_custom_call" | custom-call | tf_op jit(solution)/shard_map/pallas_call | solution.py:315
  45.0 0.6 %copy.10 = f32[8,128]{1,0:T(8,128)} copy(f32[8,128]{1,0:T(8,128)S(1)} %get-tuple-element.4) | data formatting | bytes 8192
  45.6 0.6 %copy.11 = f32[8,128]{1,0:T(8,128)} copy(f32[8,128]{1,0:T(8,128)S(1)} %get-tuple-element.5) | data formatting | bytes 8192
Async XLA Ops:
  0.6 0.7 %copy-start.4 = (f32[64]{0:T(128)S(1)}, f32[64]{0:T(128)}, u32[]{:S(2)}) copy-start(f32[64]{0:T(128)} %steps_any.1) | copy-start | bytes 772
  0.6 0.7 %copy-start.5 = (s32[8]{0:T(128)S(1)}, s32[8]{0:T(128)}, u32[]{:S(2)}) copy-start(s32[8]{0:T(128)} %ids_any.1) | copy-start | bytes 100
  1.3 0.9 %copy-start = (bf16[8,2,64,128]{3,2,1,0:T(8,128)(2,1)S(1)}, bf16[8,2,64,128]{3,2,1,0:T(8,128)(2,1)}, u32[]{:S(2)}) copy-start(bf16[8,2,64,128]{3,2,1,0:T(8,128)(2,1)} %param.6) | copy-start | bytes 786436
  2.3 0.9 %copy-start.1 = (bf16[8,2,64,128]{3,2,1,0:T(8,128)(2,1)S(1)}, bf16[8,2,64,128]{3,2,1,0:T(8,128)(2,1)}, u32[]{:S(2)}) copy-start(bf16[8,2,64,128]{3,2,1,0:T(8,128)(2,1)} %param.7) | copy-start | bytes 786436
  3.2 0.8 %copy-start.2 = (f32[128,128]{1,0:T(8,128)S(1)}, f32[128,128]{1,0:T(8,128)}, u32[]{:S(2)}) copy-start(f32[128,128]{1,0:T(8,128)} %gains_any.1) | copy-start | bytes 196612
  4.0 0.8 %copy-start.3 = (s32[128,128]{1,0:T(8,128)S(1)}, s32[128,128]{1,0:T(8,128)}, u32[]{:S(2)}) copy-start(s32[128,128]{1,0:T(8,128)} %flags_any.1) | copy-start | bytes 196612
where the time goes:
time: 46.5 us; the launch traced here: 46.2 us
  Pallas kernels  40.1 us (86%)
  local copies, waits for them, and re-layouts  5.42 us (12%)
  between operations  0.66 us (1%)
    pallas_call x1, Pallas kernels, shards(): pl.pallas_call(functools.partial(kernel, n, nchan, stations, samples), ou...  40.1 us
    unnamed x14, local copies, waits for them, and re-layouts  5.42 us

commit v1 on v0

--- a/solution.py
+++ b/solution.py
@@ -44,7 +44,8 @@
 
     def each(first, stop, body):
         if stop - first <= 16:
-            for k in range(first, stop):
+            quarter = max(stop // 4, 1)
+            for k in sorted(range(first, stop), key=lambda k: (k % quarter, (2, 1, 3, 0).index(k // quarter % 4))):
                 body(k)
         else:
             lax.fori_loop(first, stop, lambda k, carry: (body(k), carry)[1], 0)
@@ -320,7 +321,7 @@
         scratch_shapes=[pltpu.VMEM(shape, dtype) for shape, dtype in scratch]
         + [pltpu.SMEM((stations,), jnp.int32), pltpu.SemaphoreType.DMA((6,)), pltpu.SemaphoreType.DMA((GROUPS,)), pltpu.SemaphoreType.DMA((GROUPS,))],
         compiler_params=pltpu.CompilerParams(
-            collective_id=0, has_side_effects=True, vmem_limit_bytes=48 * 1024 * 1024
+            collective_id=0, has_side_effects=True, vmem_limit_bytes=64 * 1024 * 1024
         ),
     )(
         voltages.reshape(stations, samples, width),

time: 46.5 us -> 44 us (0.946)
  local copies, waits for them, and re-layouts: 5.42 us -> 1.86 us
  Pallas kernels: 40.1 us -> 41.3 us
    unnamed x14 -> x4, local copies, waits for them, and re-layouts: 5.42 us -> 1.86 us
    pallas_call x1, Pallas kernels: 40.1 us -> 41.3 us  [shards(): pl.pallas_call(functools.partial(kernel, n, nchan, stations, samples), ou...]
where the time goes in v1:
time: 44 us; the launch traced here: 43.8 us
  Pallas kernels  41.3 us (94%)
  local copies, waits for them, and re-layouts  1.86 us (4%)
  between operations  0.65 us (1%)
    pallas_call x1, Pallas kernels, shards(): pl.pallas_call(functools.partial(kernel, n, nchan, stations, samples), ou...  41.3 us
    unnamed x4, local copies, waits for them, and re-layouts  1.86 us

profile of v1, /device:TPU:0, one launch (start us, length us, event | category | flops | bytes accessed | tf_op | source)
XLA Modules:
  0.0 43.8 jit_solution(2039638409797595487)
XLA Ops:
  0.6 41.3 %shard_map.77 = (f32[8,128]{1,0:T(8,128)}, f32[8,128]{1,0:T(8,128)}) custom-call(bf16[8,128,128]{2,1,0:T(8,128)(2,1)} %bitcast.2, bf16[8,128,128]{2,1,0:T(8,128)(2,1)} %bitcast.3, f32[128,128]{1,0:T(8,128)} %gains_any.1, f32[64]{0:T(128)} %steps_any.1, s32[8]{0:T(128)} %ids_any.1, s32[128,128]{1,0:T(8,128)} %flags_any.1), custom_call_target="tpu_custom_call" | custom-call | tf_op jit(solution)/shard_map/pallas_call | solution.py:316
  41.9 0.0 copy-start
  41.9 1.3 %copy.10 = f32[8,128]{1,0:T(8,128)} copy(f32[8,128]{1,0:T(8,128)} %get-tuple-element.4) | data formatting | bytes 8192
  43.2 0.0 copy-done
  43.2 0.6 %copy.11 = f32[8,128]{1,0:T(8,128)} copy(f32[8,128]{1,0:T(8,128)S(1)} %copy-done) | data formatting | bytes 8192
Async XLA Ops:
  41.9 1.3 %copy-start = (f32[8,128]{1,0:T(8,128)S(1)}, f32[8,128]{1,0:T(8,128)}, u32[]{:S(2)}) copy-start(f32[8,128]{1,0:T(8,128)} %get-tuple-element.5) | copy-start | bytes 12292
